TPU v7x, 32 devices: a whole 2x2x4 slice. The times are simulated.
32 devices in a mesh: grid: 2 (over x), rank: 4 (over y, core), term: 4 (over z).
Axes of the slice: x: 2, y: 2, z: 4, core: 2. Of those that a mesh axis runs over, the one named last changes fastest.
Arguments:
- rhs: float32 [128, 4, 256], P('rank', 'grid')
- coef: float32 [12, 4, 256], P('term', 'grid'), may hold values from 0.03 to 0.3
- env: float32 [12, 128, 128], P('term', 'rank'), as said below
Outputs:
- solution: float32 [128, 4, 256], P('rank', 'grid')
- residual: float32 [128, 4, 256], P('rank', 'grid')
Inputs may be any that keep to these rules, and one draw needn't show every extreme that they name: env[k] is a symmetric matrix for every k.
All inputs are finite; a program needn't handle non-finite values.
Results may differ from a plain program's by a relative error of at most 0.0003.
Values sent between devices are 32-bit elements; how exact they have to be, the bound alone decides.
A program may use at most 64 MiB of HBM per device.

v0:
```python
import jax
import jax.numpy as jnp
from jax import lax
from jax.sharding import PartitionSpec as P

ITERS = 4


def padded_2(block, sides, width):
    for axis, dim in sides:
        count = lax.axis_size(axis)
        forward = [(i, i + 1) for i in range(count - 1)]
        backward = [(target, source) for source, target in forward]
        low = lax.ppermute(
            lax.slice_in_dim(block, block.shape[dim] - width, None, axis=dim), axis, forward
        )
        high = lax.ppermute(lax.slice_in_dim(block, 0, width, axis=dim), axis, backward)
        block = jnp.concatenate([low, block, high], axis=dim)
    return block


def face_weights(padded):
    wide = jnp.pad(padded, ((0, 0), (0, 0), (1, 1)))
    centre = wide[:, 1:-1, 1:-1]
    face_up = 0.5 * (centre + wide[:, 2:, 1:-1])
    face_down = 0.5 * (centre + wide[:, :-2, 1:-1])
    face_right = 0.5 * (centre + wide[:, 1:-1, 2:])
    face_left = 0.5 * (centre + wide[:, 1:-1, :-2])
    return (face_up + face_down + face_right + face_left, face_up, face_down, face_right, face_left)


def apply_faces(field, faces):
    middle = field[..., 1:-1, :]
    sideways = jnp.pad(middle, [(0, 0)] * (middle.ndim - 1) + [(1, 1)])
    total, face_up, face_down, face_right, face_left = faces
    return (
        total * middle
        - face_up * field[..., 2:, :]
        - face_down * field[..., :-2, :]
        - face_right * sideways[..., 2:]
        - face_left * sideways[..., :-2]
    )


def shards(rhs, coef, env):
    coef_padded = padded_2(coef, (("grid", 1),), 1)
    faces = tuple((weights[:, None] for weights in face_weights(coef_padded)))

    def square_sum(vector):
        return lax.psum(jnp.sum(vector * vector), ("grid", "rank"))

    solution = jnp.zeros(rhs.shape, jnp.float32)
    residual = rhs
    direction = rhs
    norm_now = square_sum(residual)
    for step in range(ITERS):
        padded = padded_2(direction, (("grid", 1),), 1)
        stenciled = apply_faces(padded[None], faces)
        image = lax.psum_scatter(
            jnp.einsum("krs,krxy->sxy", env, stenciled, precision=lax.Precision.HIGHEST),
            "rank",
            scatter_dimension=0,
            tiled=True,
        )
        image = lax.psum(image, "term")
        alpha = norm_now / lax.psum(jnp.sum(direction * image), ("grid", "rank"))
        solution = solution + alpha * direction
        residual = residual - alpha * image
        norm_next = square_sum(residual)
        direction = residual + norm_next / norm_now * direction
        norm_now = norm_next
    return (solution, residual)


def solution(mesh):
    placed = (P("rank", "grid", None), P("term", "grid", None), P("term", "rank", None))
    return jax.shard_map(
        shards,
        mesh=mesh,
        in_specs=placed,
        out_specs=(P("rank", "grid", None), P("rank", "grid", None)),
        check_vma=False,
    )
```

profile of v0, /device:TPU:0, one launch (start us, length us, event | category | flops | bytes accessed | tf_op | source)
XLA Modules:
  0.0 443.1 jit_solution(13769848011755938709)
XLA Ops:
  7.2 0.8 fusion.103
  8.0 4.8 %collective-permute-start.1 = (f32[3,1,256]{2,1,0:T(1,128)S(1)}, f32[3,1,256]{2,1,0:T(1,128)S(1)}, u32[]{:S(2)}, u32[]{:S(2)}) collective-permute-start(f32[3,1,256]{2,1,0:T(1,128)S(1)} %get-tuple-element.49), channel_id=1, source_target_pairs={{0,16},{1,17},{2,18},{3,19},{4,20},{5,21},{6,22},{7,23},{8,24},{9,... | collective-permute-start | bytes 9224 | tf_op jit(solution)/shard_map/ppermute | solution.py:14
  12.8 1.3 collective-permute-start
  14.2 1.0 fusion.102
  15.1 4.5 %collective-permute-start.2 = (f32[32,1,256]{2,1,0:T(1,128)S(1)}, f32[32,1,256]{2,1,0:T(1,128)S(1)}, u32[]{:S(2)}, u32[]{:S(2)}) collective-permute-start(f32[32,1,256]{2,1,0:T(1,128)S(1)} %get-tuple-element.47), channel_id=1, source_target_pairs={{0,16},{1,17},{2,18},{3,19},{4,20},{5,21},{6,22},{7,23},{8,24},{9,... | collective-permute-start | bytes 98312 | tf_op jit(solution)/shard_map/ppermute | solution.py:14
  19.7 1.3 collective-permute-start.3
  21.3 4.2 collective-permute-done.3
  26.6 0.8 copy.46
  27.5 0.6 copy-done.7
  29.4 30.5 %all-reduce.27.cloned.1.call-done = f32[128,2,256]{2,1,0:T(2,128)} async-done(((f32[128,2,256]{2,1,0:T(2,128)}), f32[128,2,256]{2,1,0:T(2,128)}) %all-reduce.27.cloned.1.call-update) | async-done | bytes 262160
  59.9 1.5 constant_dynamic-slice_fusion.3
  61.4 35.5 %all-reduce.19.cloned.1.call-done = f32[32,2,256]{2,1,0:T(2,128)} async-done(((f32[32,2,256]{2,1,0:T(2,128)}), f32[32,2,256]{2,1,0:T(2,128)}) %all-reduce.19.cloned.1.call-update) | async-done | bytes 65552 | tf_op jit(solution)/shard_map/psum | solution.py:65
  96.9 1.6 multiply_reduce_fusion.6
  98.5 12.5 %all-reduce.9 = (f32[]{:T(128)}, f32[]{:T(128)}) all-reduce(f32[]{:T(128)} %get-tuple-element.5, f32[]{:T(128)} %get-tuple-element.4), channel_id=1, replica_groups=mesh['grid'=2,'rank'=4,'term'=4] {'grid','rank'}, use_global_device_ids=true, to_apply=%region_1.2 | all-reduce | flops 2 | bytes 16 | tf_op jit(solution)/shard_map/psum | solution.py:50
  112.3 0.7 multiply_reduce_fusion.5
  113.0 12.5 %psum.87 = f32[]{:T(128)} all-reduce(f32[]{:T(128)} %multiply_reduce_fusion.5), channel_id=1, replica_groups=mesh['grid'=2,'rank'=4,'term'=4] {'grid','rank'}, use_global_device_ids=true, to_apply=%region_7.8 | all-reduce | flops 1 | bytes 8 | tf_op jit(solution)/shard_map/psum | solution.py:50
  126.9 3.4 collective-permute-start.4
  130.3 1.3 collective-permute-start.5
  131.9 4.2 collective-permute-done.5
  136.9 0.8 copy.50
  137.8 30.0 %all-reduce.29.cloned.1.call-done = f32[128,2,256]{2,1,0:T(2,128)} async-done(((f32[128,2,256]{2,1,0:T(2,128)}), f32[128,2,256]{2,1,0:T(2,128)}) %all-reduce.29.cloned.1.call-update) | async-done | bytes 262160
  167.8 1.5 constant_dynamic-slice_fusion.2
  169.3 35.3 %all-reduce.21.cloned.1.call-done = f32[32,2,256]{2,1,0:T(2,128)} async-done(((f32[32,2,256]{2,1,0:T(2,128)}), f32[32,2,256]{2,1,0:T(2,128)}) %all-reduce.21.cloned.1.call-update) | async-done | bytes 65552 | tf_op jit(solution)/shard_map/psum | solution.py:65
  204.6 1.6 multiply_reduce_fusion.4
  206.2 12.5 %psum.89 = f32[]{:T(128)} all-reduce(f32[]{:T(128)} %multiply_reduce_fusion.4), channel_id=1, replica_groups=mesh['grid'=2,'rank'=4,'term'=4] {'grid','rank'}, use_global_device_ids=true, to_apply=%region_11.12 | all-reduce | flops 1 | bytes 8 | tf_op jit(solution)/shard_map/psum | solution.py:66
  220.1 0.7 multiply_reduce_fusion.3
  220.7 12.4 %psum.90 = f32[]{:T(128)} all-reduce(f32[]{:T(128)} %get-tuple-element.10), channel_id=1, replica_groups=mesh['grid'=2,'rank'=4,'term'=4] {'grid','rank'}, use_global_device_ids=true, to_apply=%region_13.14 | all-reduce | flops 1 | bytes 8 | tf_op jit(solution)/shard_map/psum | solution.py:50
  234.6 3.4 collective-permute-start.6
  238.0 1.3 collective-permute-start.7
  239.6 4.2 collective-permute-done.7
  244.6 0.8 copy.54
  245.5 30.0 %all-reduce.31.cloned.1.call-done = f32[128,2,256]{2,1,0:T(2,128)} async-done(((f32[128,2,256]{2,1,0:T(2,128)}), f32[128,2,256]{2,1,0:T(2,128)}) %all-reduce.31.cloned.1.call-update) | async-done | bytes 262160
  275.4 1.5 constant_dynamic-slice_fusion.1
  277.0 35.3 %all-reduce.23.cloned.1.call-done = f32[32,2,256]{2,1,0:T(2,128)} async-done(((f32[32,2,256]{2,1,0:T(2,128)}), f32[32,2,256]{2,1,0:T(2,128)}) %all-reduce.23.cloned.1.call-update) | async-done | bytes 65552 | tf_op jit(solution)/shard_map/psum | solution.py:65
  312.3 1.6 multiply_reduce_fusion.2
  313.9 12.5 %psum.92 = f32[]{:T(128)} all-reduce(f32[]{:T(128)} %multiply_reduce_fusion.2), channel_id=1, replica_groups=mesh['grid'=2,'rank'=4,'term'=4] {'grid','rank'}, use_global_device_ids=true, to_apply=%region_17.18 | all-reduce | flops 1 | bytes 8 | tf_op jit(solution)/shard_map/psum | solution.py:66
  327.7 0.7 multiply_reduce_fusion.1
  328.4 12.5 %psum.93 = f32[]{:T(128)} all-reduce(f32[]{:T(128)} %get-tuple-element.8), channel_id=1, replica_groups=mesh['grid'=2,'rank'=4,'term'=4] {'grid','rank'}, use_global_device_ids=true, to_apply=%region_19.20 | all-reduce | flops 1 | bytes 8 | tf_op jit(solution)/shard_map/psum | solution.py:50
  342.3 3.4 collective-permute-start.8
  345.7 1.3 collective-permute-start.9
  347.3 4.2 collective-permute-done.9
  352.3 0.8 copy.58
  353.2 30.0 %all-reduce.33.cloned.1.call-done = f32[128,2,256]{2,1,0:T(2,128)} async-done(((f32[128,2,256]{2,1,0:T(2,128)}), f32[128,2,256]{2,1,0:T(2,128)}) %all-reduce.33.cloned.1.call-update) | async-done | bytes 262160
  383.1 1.5 constant_dynamic-slice_fusion
  384.6 35.5 %all-reduce.25.cloned.1.call-done = f32[32,2,256]{2,1,0:T(2,128)} async-done(((f32[32,2,256]{2,1,0:T(2,128)}), f32[32,2,256]{2,1,0:T(2,128)}) %all-reduce.25.cloned.1.call-update) | async-done | bytes 65552 | tf_op jit(solution)/shard_map/psum | solution.py:65
  420.1 1.6 multiply_reduce_fusion
  421.7 12.5 %psum.95 = f32[]{:T(128)} all-reduce(f32[]{:T(128)} %multiply_reduce_fusion), channel_id=1, replica_groups=mesh['grid'=2,'rank'=4,'term'=4] {'grid','rank'}, use_global_device_ids=true, to_apply=%region_23.24 | all-reduce | flops 1 | bytes 8 | tf_op jit(solution)/shard_map/psum | solution.py:66
  435.6 0.7 multiply_subtract_fusion
  (81 shorter events, 5.6 us)
Async XLA Ops:
  7.2 18.8 %copy-start = (f32[3,32,128]{2,1,0:T(8,128)S(1)}, f32[3,32,128]{2,1,0:T(8,128)}, u32[]{:S(2)}) copy-start(f32[3,32,128]{2,1,0:T(8,128)} %param.5) | copy-start | bytes 147460
  7.2 52.7 %all-reduce.27.cloned.1.call-start = ((), (), s32[]{:S(2)}) async-start(), calls=%async_computation.4 | async-start | bytes 524288
  8.0 13.0 %collective-permute-start.1 = (f32[3,1,256]{2,1,0:T(1,128)S(1)}, f32[3,1,256]{2,1,0:T(1,128)S(1)}, u32[]{:S(2)}, u32[]{:S(2)}) collective-permute-start(f32[3,1,256]{2,1,0:T(1,128)S(1)} %get-tuple-element.49), channel_id=1, source_target_pairs={{0,16},{1,17},{2,18},{3,19},{4,20},{5,21},{6,22},{7,23},{8,24},{9,... | collective-permute-start | bytes 9224 | tf_op jit(solution)/shard_map/ppermute | solution.py:14
  12.8 8.2 %collective-permute-start = (f32[3,1,256]{2,1,0:T(1,128)S(1)}, f32[3,1,256]{2,1,0:T(1,128)S(1)}, u32[]{:S(2)}, u32[]{:S(2)}) collective-permute-start(f32[3,1,256]{2,1,0:T(1,128)S(1)} %get-tuple-element.50), channel_id=1, source_target_pairs={{16,0},{17,1},{18,2},{19,3},{20,4},{21,5},{22,6},{23,7},{24,8},{25... | collective-permute-start | bytes 9224 | tf_op jit(solution)/shard_map/ppermute | solution.py:17
  14.1 6.9 %copy-start.6 = (f32[3,2,256]{2,1,0:T(2,128)S(1)}, f32[3,2,256]{2,1,0:T(2,128)}, u32[]{:S(2)}) copy-start(f32[3,2,256]{2,1,0:T(2,128)} %param.4) | copy-start | bytes 18436
  15.1 6.1 %collective-permute-start.2 = (f32[32,1,256]{2,1,0:T(1,128)S(1)}, f32[32,1,256]{2,1,0:T(1,128)S(1)}, u32[]{:S(2)}, u32[]{:S(2)}) collective-permute-start(f32[32,1,256]{2,1,0:T(1,128)S(1)} %get-tuple-element.47), channel_id=1, source_target_pairs={{0,16},{1,17},{2,18},{3,19},{4,20},{5,21},{6,22},{7,23},{8,24},{9,... | collective-permute-start | bytes 98312 | tf_op jit(solution)/shard_map/ppermute | solution.py:14
  19.7 5.8 %collective-permute-start.3 = (f32[32,1,256]{2,1,0:T(1,128)S(1)}, f32[32,1,256]{2,1,0:T(1,128)S(1)}, u32[]{:S(2)}, u32[]{:S(2)}) collective-permute-start(f32[32,1,256]{2,1,0:T(1,128)S(1)} %get-tuple-element.48), channel_id=1, source_target_pairs={{16,0},{17,1},{18,2},{19,3},{20,4},{21,5},{22,6},{23,7},{24,8},{25... | collective-permute-start | bytes 98312 | tf_op jit(solution)/shard_map/ppermute | solution.py:17
  21.1 4.4 copy-start.1
  27.4 69.5 %all-reduce.19.cloned.1.call-start = ((), (), s32[]{:S(2)}) async-start(), calls=%async_computation | async-start | bytes 131072 | tf_op jit(solution)/shard_map/psum | solution.py:65
  27.5 0.7 copy-start.7
  61.4 106.4 %all-reduce.29.cloned.1.call-start = ((), (), s32[]{:S(2)}) async-start(), calls=%async_computation.5 | async-start | bytes 524288
  96.9 15.4 %copy-start.2 = (f32[32,2,256]{2,1,0:T(2,128)S(1)}, f32[32,2,256]{2,1,0:T(2,128)}, u32[]{:S(2)}) copy-start(f32[32,2,256]{2,1,0:T(2,128)} %all-reduce.19.cloned.1.call-done) | copy-start | bytes 196612
  126.9 4.9 %collective-permute-start.4 = (f32[32,1,256]{2,1,0:T(1,128)S(1)}, f32[32,1,256]{2,1,0:T(1,128)S(1)}, u32[]{:S(2)}, u32[]{:S(2)}) collective-permute-start(f32[32,1,256]{2,1,0:T(1,128)S(1)} %get-tuple-element.43), channel_id=1, source_target_pairs={{0,16},{1,17},{2,18},{3,19},{4,20},{5,21},{6,22},{7,23},{8,24},{9,... | collective-permute-start | bytes 98312 | tf_op jit(solution)/shard_map/ppermute | solution.py:14
  130.3 5.8 %collective-permute-start.5 = (f32[32,1,256]{2,1,0:T(1,128)S(1)}, f32[32,1,256]{2,1,0:T(1,128)S(1)}, u32[]{:S(2)}, u32[]{:S(2)}) collective-permute-start(f32[32,1,256]{2,1,0:T(1,128)S(1)} %get-tuple-element.44), channel_id=1, source_target_pairs={{16,0},{17,1},{18,2},{19,3},{20,4},{21,5},{22,6},{23,7},{24,8},{25... | collective-permute-start | bytes 98312 | tf_op jit(solution)/shard_map/ppermute | solution.py:17
  137.7 66.9 %all-reduce.21.cloned.1.call-start = ((), (), s32[]{:S(2)}) async-start(), calls=%async_computation.1 | async-start | bytes 131072 | tf_op jit(solution)/shard_map/psum | solution.py:65
  169.2 106.2 %all-reduce.31.cloned.1.call-start = ((), (), s32[]{:S(2)}) async-start(), calls=%async_computation.6 | async-start | bytes 524288
  204.6 15.4 %copy-start.4 = (f32[32,2,256]{2,1,0:T(2,128)S(1)}, f32[32,2,256]{2,1,0:T(2,128)}, u32[]{:S(2)}) copy-start(f32[32,2,256]{2,1,0:T(2,128)} %all-reduce.21.cloned.1.call-done) | copy-start | bytes 196612
  234.6 4.9 %collective-permute-start.6 = (f32[32,1,256]{2,1,0:T(1,128)S(1)}, f32[32,1,256]{2,1,0:T(1,128)S(1)}, u32[]{:S(2)}, u32[]{:S(2)}) collective-permute-start(f32[32,1,256]{2,1,0:T(1,128)S(1)} %get-tuple-element.39), channel_id=1, source_target_pairs={{0,16},{1,17},{2,18},{3,19},{4,20},{5,21},{6,22},{7,23},{8,24},{9,... | collective-permute-start | bytes 98312 | tf_op jit(solution)/shard_map/ppermute | solution.py:14
  238.0 5.8 %collective-permute-start.7 = (f32[32,1,256]{2,1,0:T(1,128)S(1)}, f32[32,1,256]{2,1,0:T(1,128)S(1)}, u32[]{:S(2)}, u32[]{:S(2)}) collective-permute-start(f32[32,1,256]{2,1,0:T(1,128)S(1)} %get-tuple-element.40), channel_id=1, source_target_pairs={{16,0},{17,1},{18,2},{19,3},{20,4},{21,5},{22,6},{23,7},{24,8},{25... | collective-permute-start | bytes 98312 | tf_op jit(solution)/shard_map/ppermute | solution.py:17
  245.4 66.9 %all-reduce.23.cloned.1.call-start = ((), (), s32[]{:S(2)}) async-start(), calls=%async_computation.2 | async-start | bytes 131072 | tf_op jit(solution)/shard_map/psum | solution.py:65
  276.9 106.2 %all-reduce.33.cloned.1.call-start = ((), (), s32[]{:S(2)}) async-start(), calls=%async_computation.7 | async-start | bytes 524288
  312.3 15.4 %copy-start.3 = (f32[32,2,256]{2,1,0:T(2,128)S(1)}, f32[32,2,256]{2,1,0:T(2,128)}, u32[]{:S(2)}) copy-start(f32[32,2,256]{2,1,0:T(2,128)} %all-reduce.23.cloned.1.call-done) | copy-start | bytes 196612
  342.3 4.9 %collective-permute-start.8 = (f32[32,1,256]{2,1,0:T(1,128)S(1)}, f32[32,1,256]{2,1,0:T(1,128)S(1)}, u32[]{:S(2)}, u32[]{:S(2)}) collective-permute-start(f32[32,1,256]{2,1,0:T(1,128)S(1)} %get-tuple-element.35), channel_id=1, source_target_pairs={{0,16},{1,17},{2,18},{3,19},{4,20},{5,21},{6,22},{7,23},{8,24},{9,... | collective-permute-start | bytes 98312 | tf_op jit(solution)/shard_map/ppermute | solution.py:14
  345.7 5.8 %collective-permute-start.9 = (f32[32,1,256]{2,1,0:T(1,128)S(1)}, f32[32,1,256]{2,1,0:T(1,128)S(1)}, u32[]{:S(2)}, u32[]{:S(2)}) collective-permute-start(f32[32,1,256]{2,1,0:T(1,128)S(1)} %get-tuple-element.36), channel_id=1, source_target_pairs={{16,0},{17,1},{18,2},{19,3},{20,4},{21,5},{22,6},{23,7},{24,8},{25... | collective-permute-start | bytes 98312 | tf_op jit(solution)/shard_map/ppermute | solution.py:17
  353.1 67.0 %all-reduce.25.cloned.1.call-start = ((), (), s32[]{:S(2)}) async-start(), calls=%async_computation.3 | async-start | bytes 131072 | tf_op jit(solution)/shard_map/psum | solution.py:65
  420.1 15.4 %copy-start.5 = (f32[32,2,256]{2,1,0:T(2,128)S(1)}, f32[32,2,256]{2,1,0:T(2,128)}, u32[]{:S(2)}) copy-start(f32[32,2,256]{2,1,0:T(2,128)} %all-reduce.25.cloned.1.call-done) | copy-start | bytes 196612
Sparse Core Ops, SparseCore 0:
  27.6 32.2 all-reduce.26
  62.9 33.9 all-reduce.18
  137.9 29.8 all-reduce.28
  170.6 33.9 all-reduce.20
  245.5 29.8 all-reduce.30
  278.3 33.9 all-reduce.22
  353.2 29.8 all-reduce.32
  386.1 33.9 all-reduce.24
where the time goes:
time: 444 us; the launch traced here: 443 us
  waiting for transfers between devices  280 us (63%)
  blocking collectives  87.3 us (20%)
  starting transfers between devices  26.2 us (6%)
  between operations  24.8 us (6%)
  local copies, waits for them, and re-layouts  13.1 us (3%)
  other arithmetic  9.37 us (2%)
    psum x4, waiting for transfers between devices, shards(): image = lax.psum(image, 'term')  142 us
    unnamed x12, waiting for transfers between devices  121 us
    psum x4, blocking collectives, square_sum(): return lax.psum(jnp.sum(vector * vector), ('grid', 'rank'))  49.9 us
    psum x3, blocking collectives, shards(): alpha = norm_now / lax.psum(jnp.sum(direction * image), ('grid', 'rank'))  37.4 us
    ppermute x5, starting transfers between devices, padded_2(): lax.ppermute(lax.slice_in_dim(block, block.shape[dim] - width, None, axis...  19.4 us
    ppermute x5, waiting for transfers between devices, padded_2(): lax.ppermute(lax.slice_in_dim(block, 0, width, axis=dim), axis, backward)  16.9 us
  transfers between devices with their start and end apart: 18, of which 15 were waited for; matrix products, arithmetic and copies ran while one was open for 0% of the time, Pallas kernels for 0%

commit v1 on v0

--- a/solution.py
+++ b/solution.py
@@ -62,7 +62,9 @@
             scatter_dimension=0,
             tiled=True,
         )
-        image = lax.psum(image, "term")
+        image = image
+        for hop in (1, 2):
+            image = image + lax.ppermute(image, "term", [(dev, dev ^ hop) for dev in range(4)])
         alpha = norm_now / lax.psum(jnp.sum(direction * image), ("grid", "rank"))
         solution = solution + alpha * direction
         residual = residual - alpha * image

time: 444 us -> 342 us (0.77)
  waiting for transfers between devices: 280 us -> 166 us
  starting transfers between devices: 26.2 us -> 42 us
    psum x4 -> x0, waiting for transfers between devices: 142 us -> none  [shards(): image = lax.psum(image, 'term')]
    ppermute x0 -> x8, waiting for transfers between devices: none -> 22.1 us  [shards(): lax.ppermute(image, 'term', [(dev, dev ^ hop) for dev in range(4)])]
    ppermute x0 -> x8, starting transfers between devices: none -> 15.8 us  [shards(): lax.ppermute(image, 'term', [(dev, dev ^ hop) for dev in range(4)])]
    unnamed x12 -> x8, waiting for transfers between devices: 121 us -> 126 us
  transfers between devices with their start and end apart: 18 -> 22, of which waited for: 15 -> 19; matrix products, arithmetic and copies ran while one was open for 0% -> 1% of each run, Pallas kernels for 0% -> 0%
where the time goes in v1:
time: 342 us; the launch traced here: 341 us
  waiting for transfers between devices  166 us (49%)
  blocking collectives  86.9 us (25%)
  starting transfers between devices  42 us (12%)
  between operations  24.2 us (7%)
  local copies, waits for them, and re-layouts  10.6 us (3%)
  other arithmetic  9.24 us (3%)
    unnamed x8, waiting for transfers between devices  126 us
    psum x4, blocking collectives, square_sum(): return lax.psum(jnp.sum(vector * vector), ('grid', 'rank'))  49.6 us
    psum x3, blocking collectives, shards(): alpha = norm_now / lax.psum(jnp.sum(direction * image), ('grid', 'rank'))  37.2 us
    ppermute x8, waiting for transfers between devices, shards(): lax.ppermute(image, 'term', [(dev, dev ^ hop) for dev in range(4)])  22.1 us
    ppermute x5, starting transfers between devices, padded_2(): lax.ppermute(lax.slice_in_dim(block, block.shape[dim] - width, None, axis...  19.5 us
    ppermute x5, waiting for transfers between devices, padded_2(): lax.ppermute(lax.slice_in_dim(block, 0, width, axis=dim), axis, backward)  16.9 us
    ppermute x8, starting transfers between devices, shards(): lax.ppermute(image, 'term', [(dev, dev ^ hop) for dev in range(4)])  15.8 us
  transfers between devices with their start and end apart: 22, of which 19 were waited for; matrix products, arithmetic and copies ran while one was open for 1% of the time, Pallas kernels for 0%

profile of v1, /device:TPU:0, one launch (start us, length us, event | category | flops | bytes accessed | tf_op | source)
XLA Modules:
  0.0 341.4 jit_solution(9862075367703886013)
XLA Ops:
  8.0 4.8 %collective-permute-start.1 = (f32[3,1,256]{2,1,0:T(1,128)S(1)}, f32[3,1,256]{2,1,0:T(1,128)S(1)}, u32[]{:S(2)}, u32[]{:S(2)}) collective-permute-start(f32[3,1,256]{2,1,0:T(1,128)S(1)} %get-tuple-element.56), channel_id=1, source_target_pairs={{0,16},{1,17},{2,18},{3,19},{4,20},{5,21},{6,22},{7,23},{8,24},{9,... | collective-permute-start | bytes 9224 | tf_op jit(solution)/shard_map/ppermute | solution.py:14
  12.8 1.3 collective-permute-start
  14.2 1.0 fusion.102
  15.1 4.5 %collective-permute-start.2 = (f32[32,1,256]{2,1,0:T(1,128)S(1)}, f32[32,1,256]{2,1,0:T(1,128)S(1)}, u32[]{:S(2)}, u32[]{:S(2)}) collective-permute-start(f32[32,1,256]{2,1,0:T(1,128)S(1)} %get-tuple-element.54), channel_id=1, source_target_pairs={{0,16},{1,17},{2,18},{3,19},{4,20},{5,21},{6,22},{7,23},{8,24},{9,... | collective-permute-start | bytes 98312 | tf_op jit(solution)/shard_map/ppermute | solution.py:14
  19.7 1.3 collective-permute-start.3
  21.3 4.2 %collective-permute-done.3 = f32[32,1,256]{2,1,0:T(1,128)S(1)} collective-permute-done((f32[32,1,256]{2,1,0:T(1,128)S(1)}, f32[32,1,256]{2,1,0:T(1,128)S(1)}, u32[]{:S(2)}, u32[]{:S(2)}) %collective-permute-start.3) | collective-permute-done | bytes 32800 | tf_op jit(solution)/shard_map/ppermute | solution.py:17
  29.4 30.5 %all-reduce.15.cloned.1.call-done = f32[128,2,256]{2,1,0:T(2,128)} async-done(((f32[128,2,256]{2,1,0:T(2,128)}), f32[128,2,256]{2,1,0:T(2,128)}) %all-reduce.15.cloned.1.call-update) | async-done | bytes 262160
  59.9 0.8 constant_dynamic-slice_fusion.3
  60.7 1.5 collective-permute-start.4
  62.2 2.8 collective-permute-done.4
  65.0 0.9 fusion.107
  65.9 2.5 collective-permute-start.5
  68.3 2.8 collective-permute-done.5
  71.8 12.4 %all-reduce.9 = (f32[]{:T(128)}, f32[]{:T(128)}) all-reduce(f32[]{:T(128)} %get-tuple-element.5, f32[]{:T(128)} %get-tuple-element.4), channel_id=1, replica_groups=mesh['grid'=2,'rank'=4,'term'=4] {'grid','rank'}, use_global_device_ids=true, to_apply=%region_1.2 | all-reduce | flops 2 | bytes 16 | tf_op jit(solution)/shard_map/psum | solution.py:50
  86.2 12.4 %psum.58 = f32[]{:T(128)} all-reduce(f32[]{:T(128)} %multiply_reduce_fusion.5), channel_id=1, replica_groups=mesh['grid'=2,'rank'=4,'term'=4] {'grid','rank'}, use_global_device_ids=true, to_apply=%region_6.7 | all-reduce | flops 1 | bytes 8 | tf_op jit(solution)/shard_map/psum | solution.py:50
  100.1 3.4 collective-permute-start.6
  103.5 1.3 collective-permute-start.7
  105.0 4.2 %collective-permute-done.7 = f32[32,1,256]{2,1,0:T(1,128)S(1)} collective-permute-done((f32[32,1,256]{2,1,0:T(1,128)S(1)}, f32[32,1,256]{2,1,0:T(1,128)S(1)}, u32[]{:S(2)}, u32[]{:S(2)}) %collective-permute-start.7) | collective-permute-done | bytes 32800 | tf_op jit(solution)/shard_map/ppermute | solution.py:17
  110.9 31.9 %all-reduce.17.cloned.1.call-done = f32[128,2,256]{2,1,0:T(2,128)} async-done(((f32[128,2,256]{2,1,0:T(2,128)}), f32[128,2,256]{2,1,0:T(2,128)}) %all-reduce.17.cloned.1.call-update) | async-done | bytes 262160
  142.8 0.8 constant_dynamic-slice_fusion.2
  143.6 1.5 collective-permute-start.8
  145.1 2.8 collective-permute-done.8
  147.9 0.9 fusion.106
  148.8 2.5 collective-permute-start.9
  151.3 2.8 collective-permute-done.9
  154.7 12.4 %psum.59 = f32[]{:T(128)} all-reduce(f32[]{:T(128)} %get-tuple-element.16), channel_id=1, replica_groups=mesh['grid'=2,'rank'=4,'term'=4] {'grid','rank'}, use_global_device_ids=true, to_apply=%region_9.10 | all-reduce | flops 1 | bytes 8 | tf_op jit(solution)/shard_map/psum | solution.py:68
  169.1 12.4 %psum.60 = f32[]{:T(128)} all-reduce(f32[]{:T(128)} %get-tuple-element.14), channel_id=1, replica_groups=mesh['grid'=2,'rank'=4,'term'=4] {'grid','rank'}, use_global_device_ids=true, to_apply=%region_11.12 | all-reduce | flops 1 | bytes 8 | tf_op jit(solution)/shard_map/psum | solution.py:50
  182.9 3.4 collective-permute-start.10
  186.3 1.3 collective-permute-start.11
  187.9 4.2 %collective-permute-done.11 = f32[32,1,256]{2,1,0:T(1,128)S(1)} collective-permute-done((f32[32,1,256]{2,1,0:T(1,128)S(1)}, f32[32,1,256]{2,1,0:T(1,128)S(1)}, u32[]{:S(2)}, u32[]{:S(2)}) %collective-permute-start.11) | collective-permute-done | bytes 32800 | tf_op jit(solution)/shard_map/ppermute | solution.py:17
  193.8 31.8 %all-reduce.19.cloned.1.call-done = f32[128,2,256]{2,1,0:T(2,128)} async-done(((f32[128,2,256]{2,1,0:T(2,128)}), f32[128,2,256]{2,1,0:T(2,128)}) %all-reduce.19.cloned.1.call-update) | async-done | bytes 262160
  226.5 1.5 collective-permute-start.12
  228.0 2.8 collective-permute-done.12
  230.8 0.9 fusion.105
  231.7 2.5 collective-permute-start.13
  234.1 2.8 collective-permute-done.13
  237.6 12.4 %psum.61 = f32[]{:T(128)} all-reduce(f32[]{:T(128)} %get-tuple-element.12), channel_id=1, replica_groups=mesh['grid'=2,'rank'=4,'term'=4] {'grid','rank'}, use_global_device_ids=true, to_apply=%region_14.15 | all-reduce | flops 1 | bytes 8 | tf_op jit(solution)/shard_map/psum | solution.py:68
  252.0 12.4 %psum.62 = f32[]{:T(128)} all-reduce(f32[]{:T(128)} %get-tuple-element.10), channel_id=1, replica_groups=mesh['grid'=2,'rank'=4,'term'=4] {'grid','rank'}, use_global_device_ids=true, to_apply=%region_16.17 | all-reduce | flops 1 | bytes 8 | tf_op jit(solution)/shard_map/psum | solution.py:50
  265.8 3.4 collective-permute-start.14
  269.2 1.3 collective-permute-start.15
  270.8 4.2 %collective-permute-done.15 = f32[32,1,256]{2,1,0:T(1,128)S(1)} collective-permute-done((f32[32,1,256]{2,1,0:T(1,128)S(1)}, f32[32,1,256]{2,1,0:T(1,128)S(1)}, u32[]{:S(2)}, u32[]{:S(2)}) %collective-permute-start.15) | collective-permute-done | bytes 32800 | tf_op jit(solution)/shard_map/ppermute | solution.py:17
  276.7 31.9 %all-reduce.21.cloned.1.call-done = f32[128,2,256]{2,1,0:T(2,128)} async-done(((f32[128,2,256]{2,1,0:T(2,128)}), f32[128,2,256]{2,1,0:T(2,128)}) %all-reduce.21.cloned.1.call-update) | async-done | bytes 262160
  309.4 1.5 collective-permute-start.16
  310.9 2.8 collective-permute-done.16
  313.7 0.9 fusion.104
  314.5 2.5 collective-permute-start.17
  317.0 2.8 collective-permute-done.17
  320.4 12.4 %psum.63 = f32[]{:T(128)} all-reduce(f32[]{:T(128)} %get-tuple-element.8), channel_id=1, replica_groups=mesh['grid'=2,'rank'=4,'term'=4] {'grid','rank'}, use_global_device_ids=true, to_apply=%region_19.20 | all-reduce | flops 1 | bytes 8 | tf_op jit(solution)/shard_map/psum | solution.py:68
  (81 shorter events, 17.2 us)
Async XLA Ops:
  7.2 18.8 %copy-start = (f32[3,32,128]{2,1,0:T(8,128)S(1)}, f32[3,32,128]{2,1,0:T(8,128)}, u32[]{:S(2)}) copy-start(f32[3,32,128]{2,1,0:T(8,128)} %param.5) | copy-start | bytes 147460
  7.2 52.7 %all-reduce.15.cloned.1.call-start = ((), (), s32[]{:S(2)}) async-start(), calls=%async_computation | async-start | bytes 524288
  8.0 13.0 %collective-permute-start.1 = (f32[3,1,256]{2,1,0:T(1,128)S(1)}, f32[3,1,256]{2,1,0:T(1,128)S(1)}, u32[]{:S(2)}, u32[]{:S(2)}) collective-permute-start(f32[3,1,256]{2,1,0:T(1,128)S(1)} %get-tuple-element.56), channel_id=1, source_target_pairs={{0,16},{1,17},{2,18},{3,19},{4,20},{5,21},{6,22},{7,23},{8,24},{9,... | collective-permute-start | bytes 9224 | tf_op jit(solution)/shard_map/ppermute | solution.py:14
  12.8 8.2 %collective-permute-start = (f32[3,1,256]{2,1,0:T(1,128)S(1)}, f32[3,1,256]{2,1,0:T(1,128)S(1)}, u32[]{:S(2)}, u32[]{:S(2)}) collective-permute-start(f32[3,1,256]{2,1,0:T(1,128)S(1)} %get-tuple-element.57), channel_id=1, source_target_pairs={{16,0},{17,1},{18,2},{19,3},{20,4},{21,5},{22,6},{23,7},{24,8},{25... | collective-permute-start | bytes 9224 | tf_op jit(solution)/shard_map/ppermute | solution.py:17
  14.1 6.9 %copy-start.2 = (f32[3,2,256]{2,1,0:T(2,128)S(1)}, f32[3,2,256]{2,1,0:T(2,128)}, u32[]{:S(2)}) copy-start(f32[3,2,256]{2,1,0:T(2,128)} %param.4) | copy-start | bytes 18436
  15.1 6.1 %collective-permute-start.2 = (f32[32,1,256]{2,1,0:T(1,128)S(1)}, f32[32,1,256]{2,1,0:T(1,128)S(1)}, u32[]{:S(2)}, u32[]{:S(2)}) collective-permute-start(f32[32,1,256]{2,1,0:T(1,128)S(1)} %get-tuple-element.54), channel_id=1, source_target_pairs={{0,16},{1,17},{2,18},{3,19},{4,20},{5,21},{6,22},{7,23},{8,24},{9,... | collective-permute-start | bytes 98312 | tf_op jit(solution)/shard_map/ppermute | solution.py:14
  19.7 5.8 %collective-permute-start.3 = (f32[32,1,256]{2,1,0:T(1,128)S(1)}, f32[32,1,256]{2,1,0:T(1,128)S(1)}, u32[]{:S(2)}, u32[]{:S(2)}) collective-permute-start(f32[32,1,256]{2,1,0:T(1,128)S(1)} %get-tuple-element.55), channel_id=1, source_target_pairs={{16,0},{17,1},{18,2},{19,3},{20,4},{21,5},{22,6},{23,7},{24,8},{25... | collective-permute-start | bytes 98312 | tf_op jit(solution)/shard_map/ppermute | solution.py:17
  21.1 4.4 %copy-start.1 = (f32[32,2,256]{2,1,0:T(2,128)S(1)}, f32[32,2,256]{2,1,0:T(2,128)}, u32[]{:S(2)}) copy-start(f32[32,2,256]{2,1,0:T(2,128)} %param.3) | copy-start | bytes 196612
  27.4 115.4 %all-reduce.17.cloned.1.call-start = ((), (), s32[]{:S(2)}) async-start(), calls=%async_computation.1 | async-start | bytes 524288
  27.5 0.7 copy-start.3
  60.7 4.3 %collective-permute-start.4 = (f32[32,2,256]{2,1,0:T(2,128)S(1)}, f32[32,2,256]{2,1,0:T(2,128)S(1)}, u32[]{:S(2)}, u32[]{:S(2)}) collective-permute-start(f32[32,2,256]{2,1,0:T(2,128)S(1)} %constant_dynamic-slice_fusion.3), channel_id=1, source_target_pairs={{0,1},{1,0},{2,3},{3,2},{4,5},{5,4},{6,7},{7,6},{8,9},{9,8},{10,11... | collective-permute-start | bytes 196616 | tf_op jit(solution)/shard_map/ppermute | solution.py:67
  65.9 5.2 %collective-permute-start.5 = (f32[32,2,256]{2,1,0:T(2,128)S(1)}, f32[32,2,256]{2,1,0:T(2,128)S(1)}, u32[]{:S(2)}, u32[]{:S(2)}) collective-permute-start(f32[32,2,256]{2,1,0:T(2,128)S(1)} %fusion.107), channel_id=1, source_target_pairs={{0,2},{1,3},{2,0},{3,1},{4,6},{5,7},{6,4},{7,5},{8,10},{9,11},{10,... | collective-permute-start | bytes 196616 | tf_op jit(solution)/shard_map/ppermute | solution.py:67
  100.1 5.0 %collective-permute-start.6 = (f32[32,1,256]{2,1,0:T(1,128)S(1)}, f32[32,1,256]{2,1,0:T(1,128)S(1)}, u32[]{:S(2)}, u32[]{:S(2)}) collective-permute-start(f32[32,1,256]{2,1,0:T(1,128)S(1)} %get-tuple-element.50), channel_id=1, source_target_pairs={{0,16},{1,17},{2,18},{3,19},{4,20},{5,21},{6,22},{7,23},{8,24},{9,... | collective-permute-start | bytes 98312 | tf_op jit(solution)/shard_map/ppermute | solution.py:14
  103.5 5.8 %collective-permute-start.7 = (f32[32,1,256]{2,1,0:T(1,128)S(1)}, f32[32,1,256]{2,1,0:T(1,128)S(1)}, u32[]{:S(2)}, u32[]{:S(2)}) collective-permute-start(f32[32,1,256]{2,1,0:T(1,128)S(1)} %get-tuple-element.51), channel_id=1, source_target_pairs={{16,0},{17,1},{18,2},{19,3},{20,4},{21,5},{22,6},{23,7},{24,8},{25... | collective-permute-start | bytes 98312 | tf_op jit(solution)/shard_map/ppermute | solution.py:17
  110.9 114.8 %all-reduce.19.cloned.1.call-start = ((), (), s32[]{:S(2)}) async-start(), calls=%async_computation.2 | async-start | bytes 524288
  143.6 4.3 %collective-permute-start.8 = (f32[32,2,256]{2,1,0:T(2,128)S(1)}, f32[32,2,256]{2,1,0:T(2,128)S(1)}, u32[]{:S(2)}, u32[]{:S(2)}) collective-permute-start(f32[32,2,256]{2,1,0:T(2,128)S(1)} %constant_dynamic-slice_fusion.2), channel_id=1, source_target_pairs={{0,1},{1,0},{2,3},{3,2},{4,5},{5,4},{6,7},{7,6},{8,9},{9,8},{10,11... | collective-permute-start | bytes 196616 | tf_op jit(solution)/shard_map/ppermute | solution.py:67
  148.8 5.2 %collective-permute-start.9 = (f32[32,2,256]{2,1,0:T(2,128)S(1)}, f32[32,2,256]{2,1,0:T(2,128)S(1)}, u32[]{:S(2)}, u32[]{:S(2)}) collective-permute-start(f32[32,2,256]{2,1,0:T(2,128)S(1)} %fusion.106), channel_id=1, source_target_pairs={{0,2},{1,3},{2,0},{3,1},{4,6},{5,7},{6,4},{7,5},{8,10},{9,11},{10,... | collective-permute-start | bytes 196616 | tf_op jit(solution)/shard_map/ppermute | solution.py:67
  182.9 5.0 %collective-permute-start.10 = (f32[32,1,256]{2,1,0:T(1,128)S(1)}, f32[32,1,256]{2,1,0:T(1,128)S(1)}, u32[]{:S(2)}, u32[]{:S(2)}) collective-permute-start(f32[32,1,256]{2,1,0:T(1,128)S(1)} %get-tuple-element.46), channel_id=1, source_target_pairs={{0,16},{1,17},{2,18},{3,19},{4,20},{5,21},{6,22},{7,23},{8,24},{9,... | collective-permute-start | bytes 98312 | tf_op jit(solution)/shard_map/ppermute | solution.py:14
  186.3 5.8 %collective-permute-start.11 = (f32[32,1,256]{2,1,0:T(1,128)S(1)}, f32[32,1,256]{2,1,0:T(1,128)S(1)}, u32[]{:S(2)}, u32[]{:S(2)}) collective-permute-start(f32[32,1,256]{2,1,0:T(1,128)S(1)} %get-tuple-element.47), channel_id=1, source_target_pairs={{16,0},{17,1},{18,2},{19,3},{20,4},{21,5},{22,6},{23,7},{24,8},{25... | collective-permute-start | bytes 98312 | tf_op jit(solution)/shard_map/ppermute | solution.py:17
  193.8 114.8 %all-reduce.21.cloned.1.call-start = ((), (), s32[]{:S(2)}) async-start(), calls=%async_computation.3 | async-start | bytes 524288
  226.5 4.3 %collective-permute-start.12 = (f32[32,2,256]{2,1,0:T(2,128)S(1)}, f32[32,2,256]{2,1,0:T(2,128)S(1)}, u32[]{:S(2)}, u32[]{:S(2)}) collective-permute-start(f32[32,2,256]{2,1,0:T(2,128)S(1)} %constant_dynamic-slice_fusion.1), channel_id=1, source_target_pairs={{0,1},{1,0},{2,3},{3,2},{4,5},{5,4},{6,7},{7,6},{8,9},{9,8},{10,11... | collective-permute-start | bytes 196616 | tf_op jit(solution)/shard_map/ppermute | solution.py:67
  231.7 5.2 %collective-permute-start.13 = (f32[32,2,256]{2,1,0:T(2,128)S(1)}, f32[32,2,256]{2,1,0:T(2,128)S(1)}, u32[]{:S(2)}, u32[]{:S(2)}) collective-permute-start(f32[32,2,256]{2,1,0:T(2,128)S(1)} %fusion.105), channel_id=1, source_target_pairs={{0,2},{1,3},{2,0},{3,1},{4,6},{5,7},{6,4},{7,5},{8,10},{9,11},{10,... | collective-permute-start | bytes 196616 | tf_op jit(solution)/shard_map/ppermute | solution.py:67
  265.8 5.0 %collective-permute-start.14 = (f32[32,1,256]{2,1,0:T(1,128)S(1)}, f32[32,1,256]{2,1,0:T(1,128)S(1)}, u32[]{:S(2)}, u32[]{:S(2)}) collective-permute-start(f32[32,1,256]{2,1,0:T(1,128)S(1)} %get-tuple-element.42), channel_id=1, source_target_pairs={{0,16},{1,17},{2,18},{3,19},{4,20},{5,21},{6,22},{7,23},{8,24},{9,... | collective-permute-start | bytes 98312 | tf_op jit(solution)/shard_map/ppermute | solution.py:14
  269.2 5.8 %collective-permute-start.15 = (f32[32,1,256]{2,1,0:T(1,128)S(1)}, f32[32,1,256]{2,1,0:T(1,128)S(1)}, u32[]{:S(2)}, u32[]{:S(2)}) collective-permute-start(f32[32,1,256]{2,1,0:T(1,128)S(1)} %get-tuple-element.43), channel_id=1, source_target_pairs={{16,0},{17,1},{18,2},{19,3},{20,4},{21,5},{22,6},{23,7},{24,8},{25... | collective-permute-start | bytes 98312 | tf_op jit(solution)/shard_map/ppermute | solution.py:17
  309.4 4.3 %collective-permute-start.16 = (f32[32,2,256]{2,1,0:T(2,128)S(1)}, f32[32,2,256]{2,1,0:T(2,128)S(1)}, u32[]{:S(2)}, u32[]{:S(2)}) collective-permute-start(f32[32,2,256]{2,1,0:T(2,128)S(1)} %constant_dynamic-slice_fusion), channel_id=1, source_target_pairs={{0,1},{1,0},{2,3},{3,2},{4,5},{5,4},{6,7},{7,6},{8,9},{9,8},{10,11... | collective-permute-start | bytes 196616 | tf_op jit(solution)/shard_map/ppermute | solution.py:67
  314.5 5.2 %collective-permute-start.17 = (f32[32,2,256]{2,1,0:T(2,128)S(1)}, f32[32,2,256]{2,1,0:T(2,128)S(1)}, u32[]{:S(2)}, u32[]{:S(2)}) collective-permute-start(f32[32,2,256]{2,1,0:T(2,128)S(1)} %fusion.104), channel_id=1, source_target_pairs={{0,2},{1,3},{2,0},{3,1},{4,6},{5,7},{6,4},{7,5},{8,10},{9,11},{10,... | collective-permute-start | bytes 196616 | tf_op jit(solution)/shard_map/ppermute | solution.py:67
Sparse Core Ops, SparseCore 0:
  27.6 32.2 all-reduce.14
  111.0 31.7 all-reduce.16
  193.9 31.7 all-reduce.18
  276.8 31.7 all-reduce.20
